TPU v7x, 32 devices: a whole 2x2x4 slice. The times are simulated.
32 devices in a mesh: section: 2 (over core), seq: 8 (over z, x), wshard: 2 (over y).
Axes of the slice: x: 2, y: 2, z: 4, core: 2. Of those that a mesh axis runs over, the one named last changes fastest.
Arguments:
- inputs: bfloat16 [2, 2, 2048, 1024], P(None, 'wshard', 'seq'), may hold values from -6 to 6
- cotangent: bfloat16 [2, 2, 2048, 1024], P(None, 'wshard', 'seq'), may hold values from -6 to 6
- boundary: int32 [2, 2], P(None, 'wshard'), may hold values from 1024 to 2048, as said below
- norm_gain: float32 [2, 1024], P('section', 'wshard'), may hold values from 0.1 to 1.9
- w_in: bfloat16 [2, 1024, 4384], P('section', 'wshard'), may hold values from -0.1875 to 0.1875
- conv_w: float32 [2, 4, 2304], P('section', None, 'wshard'), may hold values from -3 to 3
- conv_b: float32 [2, 2304], P('section', 'wshard'), may hold values from -3 to 3
- dt_bias: float32 [2, 32], P('section', 'wshard'), may hold values from -5 to -3
- a_log: float32 [2, 32], P('section', 'wshard'), may hold values from -12 to 1
- skip_gain: float32 [2, 32], P('section', 'wshard'), may hold values from 0.5 to 1.5
- gate_norm: float32 [2, 2048], P('section', 'wshard'), may hold values from 0.1 to 1.9
- w_out: bfloat16 [2, 2048, 1024], P('section', 'wshard'), may hold values from -0.125 to 0.125
Outputs:
- acts: bfloat16 [2, 2, 2, 2048, 1024], P('section', None, 'wshard', 'seq')
- in_grad: float32 [2, 2, 2, 2048, 1024], P('section', None, 'wshard', 'seq')
- grad_norm_gain: float32 [2, 1024], P('section', 'wshard')
- grad_w_in: float32 [2, 1024, 4384], P('section', 'wshard')
- grad_conv_w: float32 [2, 4, 2304], P('section', None, 'wshard')
- grad_conv_b: float32 [2, 2304], P('section', 'wshard')
- grad_dt_bias: float32 [2, 32], P('section', 'wshard')
- grad_a_log: float32 [2, 32], P('section', 'wshard')
- grad_skip_gain: float32 [2, 32], P('section', 'wshard')
- grad_gate_norm: float32 [2, 2048], P('section', 'wshard')
- grad_w_out: float32 [2, 2048, 1024], P('section', 'wshard')
Inputs may be any that keep to these rules, and one draw needn't show every extreme that they name: `boundary`: for every stream index one micro-batch, drawn from the seed, holds one sequence of 2048 tokens and has the value 2048; every other holds two sequences, the second starting at the given position.
All inputs are finite; a program needn't handle non-finite values.
Results may differ from a plain program's by a relative error of at most 0.015.
The roundings to bfloat16 on the way count: a program that leaves them out, or rounds other values in their place, can miss the bound.
Values may be sent and summed in bfloat16 or wider, within the bound.
No kernel may reach another device: no remote copies, remote signals or barrier semaphores. Data moves between devices by JAX's collectives and lax.ppermute only.
A program may use at most 320 MiB of HBM per device.

v0:
```python
import jax
import jax.numpy as jnp
from jax import lax
from jax.sharding import PartitionSpec as P

D = 1024
DI = 2048
H = 32
N = 128
K = 4
CH = 256
DCONV = 2304


EPSILON = 1e-05


def from_behind(block, axis, distance):
    devices = range(lax.axis_size(axis))
    route = [(i - distance, i) for i in devices if i - distance in devices]
    return lax.ppermute(block, axis, route)


def carried_in(part, axis, combine, identity):
    place = lax.axis_index(axis)
    gathered = jax.tree.map(lambda a: lax.all_gather(a, axis), part)
    state = jax.tree.map(lambda a, e: jnp.zeros_like(a) + jnp.asarray(e, a.dtype), part, identity)

    def carried_one(step, state):
        return combine(
            state, jax.tree.map(lambda a: lax.dynamic_index_in_dim(a, step, 0, False), gathered)
        )

    return lax.fori_loop(0, place, carried_one, state)


def entering_2(value, axis, join, neutral):
    count = lax.axis_size(axis)
    place = lax.axis_index(axis)
    ahead = count - 1 - place
    gathered = jax.tree.map(
        lambda a, kind: lax.all_gather(a.astype(kind), axis),
        value,
        jax.tree.map(lambda a: jnp.bfloat16 if a.dtype == jnp.float32 else a.dtype, value),
    )
    state = jax.tree.map(lambda a, e: jnp.zeros_like(a) + jnp.asarray(e, a.dtype), value, neutral)

    def entering_one(step, state):
        source = count - 1 - step
        return join(
            state,
            jax.tree.map(
                lambda a, own: lax.dynamic_index_in_dim(a, source, 0, False).astype(own.dtype),
                gathered,
                value,
            ),
        )

    return lax.fori_loop(0, ahead, entering_one, state)


def rms_scale(values, gain):
    mean_square = jnp.mean(values * values, axis=-1, keepdims=True)
    return values * lax.rsqrt(mean_square + EPSILON) * gain


def group_step(carried, block_in):
    state_now, last_segment, running = carried
    inner_x, in_b, out_c, step_size, log_decay, segment = block_in
    cumulated = jnp.cumsum(log_decay, axis=0)
    length = segment.shape[0]
    places = jnp.arange(length)
    within = (places[:, None] >= places[None, :]) & (segment[:, None] == segment[None, :])
    spread = cumulated[:, None, :] - cumulated[None, :, :]
    decays = jnp.where(within[:, :, None], jnp.exp(jnp.where(within[:, :, None], spread, 0.0)), 0.0)
    scores = jnp.dot(out_c, in_b.T, precision=lax.Precision.HIGHEST)
    scaled_x = inner_x * step_size[:, :, None]
    output = jnp.einsum(
        "tsh,shp->thp", decays * scores[:, :, None], scaled_x, precision=lax.Precision.HIGHEST
    )
    entering = jnp.exp(cumulated) * (segment == last_segment).astype(jnp.float32)[:, None]
    output = output + entering[:, :, None] * jnp.einsum(
        "tn,hpn->thp", out_c, state_now, precision=lax.Precision.HIGHEST
    )
    to_end = jnp.where(
        (segment == segment[-1])[:, None], jnp.exp(cumulated[-1][None, :] - cumulated), 0.0
    )
    new_state = entering[-1][:, None, None] * state_now + jnp.einsum(
        "sh,sn,shp->hpn", to_end, in_b, scaled_x, precision=lax.Precision.HIGHEST
    )
    return ((new_state, segment[-1], running * entering[-1]), (output, running[None, :] * entering))


def ssd_scan(inner_x, in_b, out_c, step_size, log_decay, segment, first_state, last_segment):
    summed = inner_x.shape[0]
    blocks_count = summed // CH

    def split_blocks(array_in):
        return array_in.reshape((blocks_count, CH) + array_in.shape[1:])

    start_carry = (first_state, last_segment, jnp.ones((inner_x.shape[1],), jnp.float32))
    ending, (outputs, reach) = lax.scan(
        jax.checkpoint(group_step),
        start_carry,
        tuple(
            (
                split_blocks(array_in)
                for array_in in (inner_x, in_b, out_c, step_size, log_decay, segment)
            )
        ),
    )
    return (outputs.reshape(inner_x.shape), ending[0], reach.reshape(summed, inner_x.shape[1]))


def mixer_inputs(conv_pre, dt_raw, dt_bias, a_log):
    activated = jax.nn.silu(conv_pre)
    inner_x = activated[:, :DI].reshape(activated.shape[0], H, DI // H)
    in_b = activated[:, DI : DI + N]
    out_c = activated[:, DI + N :]
    step_size = jax.nn.softplus(dt_raw + dt_bias)
    log_decay = -step_size * jnp.exp(a_log)
    return (inner_x, in_b, out_c, step_size, log_decay)


def conv_piece(extended, conv_w, conv_b, tap_masks):
    length = extended.shape[0] - (K - 1)
    summed = conv_b[None, :]
    for tap_index in range(K):
        summed = (
            summed
            + conv_w[tap_index][None, :]
            * extended[tap_index : tap_index + length]
            * tap_masks[tap_index][:, None]
        )
    return summed


def ssd_piece(conv_pre, dt_raw, dt_bias, a_log, skip_gain, entry_state, segment, before):
    inner_x, in_b, out_c, step_size, log_decay = mixer_inputs(conv_pre, dt_raw, dt_bias, a_log)
    zero_state = jnp.zeros((H, DI // H, N), jnp.float32)
    output, local_state, reach = ssd_scan(
        inner_x, in_b, out_c, step_size, log_decay, segment, zero_state, before
    )
    output = output + reach[:, :, None] * jnp.einsum(
        "tn,hpn->thp", out_c, entry_state, precision=lax.Precision.HIGHEST
    )
    output = output + skip_gain[None, :, None] * inner_x
    final_state = reach[-1][:, None, None] * entry_state + local_state
    return ((output.reshape(output.shape[0], DI), final_state), (reach, out_c))


def gate_piece(mixed, gate_raw, gate_norm):
    return rms_scale(mixed * jax.nn.silu(gate_raw), gate_norm)


def state_chain(earlier, later):
    return (earlier[0] * later[0], later[0][:, None, None] * earlier[1] + later[1])


def on_device(
    inputs,
    cotangent,
    boundary,
    norm_gain,
    w_in,
    conv_w,
    conv_b,
    dt_bias,
    a_log,
    skip_gain,
    gate_norm,
    w_out,
):
    section_index = lax.axis_index("section")
    seq_index = lax.axis_index("seq")
    tokens_dev = inputs.shape[2]
    batches = inputs.shape[0]
    offset = seq_index * tokens_dev
    edge_rows = K - 1
    head_size = DI // H
    big_in, big_out = (
        lax.all_gather(w_in, "wshard", axis=1, tiled=True),
        lax.all_gather(w_out, "wshard", axis=1, tiled=True),
    )
    gathered_small = (
        lax.all_gather(norm_gain, "wshard", axis=1, tiled=True),
        lax.all_gather(conv_w, "wshard", axis=2, tiled=True),
        lax.all_gather(conv_b, "wshard", axis=1, tiled=True),
        lax.all_gather(dt_bias, "wshard", axis=1, tiled=True),
        lax.all_gather(a_log, "wshard", axis=1, tiled=True),
        lax.all_gather(skip_gain, "wshard", axis=1, tiled=True),
        lax.all_gather(gate_norm, "wshard", axis=1, tiled=True),
    )
    proj_w = big_in[0]
    out_w = big_out[0]
    gain_pre, conv_weight, conv_bias, bias_dt, log_rate, skip_heads, gain_gate = [
        member[0] for member in gathered_small
    ]
    limits = boundary[:, 0]
    positions = offset + jnp.arange(tokens_dev, dtype=jnp.int32)
    chain_identity = (jnp.ones((H,), jnp.float32), jnp.zeros((H, head_size, N), jnp.float32))

    def layout(boundary_at):
        segment = (positions >= boundary_at).astype(jnp.float32)
        before = (offset - 1 >= boundary_at).astype(jnp.float32)
        tap_masks = jnp.stack(
            [
                (
                    (positions - (edge_rows - tap_index) >= boundary_at)
                    == (positions >= boundary_at)
                ).astype(jnp.float32)
                for tap_index in range(K)
            ]
        )
        return (segment, before, tap_masks)

    def projection(normed_low):
        projected = jnp.dot(normed_low, proj_w, preferred_element_type=jnp.float32)
        return (projected[:, :DI], projected[:, DI : DI + DCONV], projected[:, DI + DCONV :])

    received = jnp.zeros((tokens_dev, D), jnp.bfloat16)
    kept_hidden = []
    kept_edges = []
    kept_entries = []
    results = []
    for tick_index in range(batches + 1):
        batch_now = jnp.clip(tick_index - section_index, 0, batches - 1)
        boundary_at = lax.dynamic_index_in_dim(limits, batch_now, keepdims=False)
        fresh = inputs[min(tick_index, batches - 1), 0]
        hidden_low = jnp.where(section_index == 0, fresh, received)
        hidden = hidden_low.astype(jnp.float32)
        segment, before, tap_masks = layout(boundary_at)
        normed_low = rms_scale(hidden, gain_pre).astype(jnp.bfloat16)
        gate_raw, conv_in, dt_raw = projection(normed_low)
        edge_in = from_behind(conv_in[tokens_dev - edge_rows :], "seq", 1)
        conv_pre = conv_piece(
            jnp.concatenate([edge_in, conv_in], axis=0), conv_weight, conv_bias, tap_masks
        )
        zero_entry = jnp.zeros((H, head_size, N), jnp.float32)
        (mixed_local, local_state), (reach, out_c) = ssd_piece(
            conv_pre, dt_raw, bias_dt, log_rate, skip_heads, zero_entry, segment, before
        )
        through, entry_state = carried_in(
            (reach[-1], local_state), "seq", state_chain, chain_identity
        )
        mixed = mixed_local + (
            reach[:, :, None]
            * jnp.einsum("tn,hpn->thp", out_c, entry_state, precision=lax.Precision.HIGHEST)
        ).reshape(tokens_dev, DI)
        gated_low = gate_piece(mixed, gate_raw, gain_gate).astype(jnp.bfloat16)
        result_low = (
            hidden + jnp.dot(gated_low, out_w, preferred_element_type=jnp.float32)
        ).astype(jnp.bfloat16)
        results.append(result_low)
        kept_hidden.append(hidden_low)
        kept_edges.append(edge_in)
        kept_entries.append(entry_state)
        received = from_behind(result_low, "section", 1)
    stacked_results = jnp.stack(results)
    hidden_all = jnp.stack(kept_hidden)
    edges_all = jnp.stack(kept_edges)
    entries_all = jnp.stack(kept_entries)
    grad_proj_w = jnp.zeros(proj_w.shape, jnp.float32)
    grad_out_w = jnp.zeros(out_w.shape, jnp.float32)
    grad_gain_pre = jnp.zeros(gain_pre.shape, jnp.float32)
    grad_conv_weight = jnp.zeros(conv_weight.shape, jnp.float32)
    grad_conv_bias = jnp.zeros(conv_bias.shape, jnp.float32)
    grad_bias_dt = jnp.zeros(bias_dt.shape, jnp.float32)
    grad_log_rate = jnp.zeros(log_rate.shape, jnp.float32)
    grad_skip_heads = jnp.zeros(skip_heads.shape, jnp.float32)
    grad_gain_gate = jnp.zeros(gain_gate.shape, jnp.float32)
    received_back = jnp.zeros((tokens_dev, D), jnp.bfloat16)
    input_grads = []
    for tick_index in range(batches + 1):
        batch_raw = batches - tick_index - section_index
        is_valid = ((batch_raw >= 0) & (batch_raw < batches)).astype(jnp.float32)
        batch_now = jnp.clip(batch_raw, 0, batches - 1)
        forward_tick = batch_now + section_index
        boundary_at = lax.dynamic_index_in_dim(limits, batch_now, keepdims=False)
        hidden = lax.dynamic_index_in_dim(hidden_all, forward_tick, keepdims=False).astype(
            jnp.float32
        )
        edge_in = lax.dynamic_index_in_dim(edges_all, forward_tick, keepdims=False)
        entry_state = lax.dynamic_index_in_dim(entries_all, forward_tick, keepdims=False)
        upstream = lax.dynamic_index_in_dim(cotangent[:, 0], batch_now, keepdims=False)
        grad_low = jnp.where(section_index == 1, upstream, received_back)
        grad_result = grad_low.astype(jnp.float32)
        segment, before, tap_masks = layout(boundary_at)
        normed, pull_norm = jax.vjp(rms_scale, hidden, gain_pre)
        normed_low = normed.astype(jnp.bfloat16)
        gate_raw, conv_in, dt_raw = projection(normed_low)

        def conv_local(extended, weight_taps, bias_taps):
            return conv_piece(extended, weight_taps, bias_taps, tap_masks)

        conv_pre, pull_conv = jax.vjp(
            conv_local, jnp.concatenate([edge_in, conv_in], axis=0), conv_weight, conv_bias
        )

        def ssd_local(
            pre_values, raw_values, bias_values, rate_values, skip_values, entering_state
        ):
            return ssd_piece(
                pre_values,
                raw_values,
                bias_values,
                rate_values,
                skip_values,
                entering_state,
                segment,
                before,
            )

        (mixed, final_state), pull_mix, (reach, out_c) = jax.vjp(
            ssd_local, conv_pre, dt_raw, bias_dt, log_rate, skip_heads, entry_state, has_aux=True
        )
        gated, pull_gate = jax.vjp(gate_piece, mixed, gate_raw, gain_gate)
        gated_low = gated.astype(jnp.bfloat16)
        term_out_w = jnp.einsum(
            "tk,td->kd", gated_low, grad_low, preferred_element_type=jnp.float32
        )
        grad_gated = jnp.dot(grad_low, out_w.T, preferred_element_type=jnp.float32)
        grad_mixed, grad_gate_raw, term_gain_gate = pull_gate(grad_gated)
        local_pull = jnp.einsum(
            "th,tn,thp->hpn",
            reach,
            out_c,
            grad_mixed.reshape(tokens_dev, H, head_size),
            precision=lax.Precision.HIGHEST,
        )
        through_back, later_grad = entering_2(
            (reach[-1], local_pull), "seq", state_chain, chain_identity
        )
        grad_pre, grad_dt_raw, term_bias_dt, term_log_rate, term_skip, unused_entry = pull_mix(
            (grad_mixed, later_grad)
        )
        grad_ext, term_conv_weight, term_conv_bias = pull_conv(grad_pre)
        edge_back = from_behind(grad_ext[:edge_rows], "seq", -1)
        grad_conv_in = grad_ext[edge_rows:] + jnp.concatenate(
            [jnp.zeros((tokens_dev - edge_rows, DCONV), jnp.float32), edge_back], axis=0
        )
        grad_proj = jnp.concatenate([grad_gate_raw, grad_conv_in, grad_dt_raw], axis=1).astype(
            jnp.bfloat16
        )
        term_proj_w = jnp.einsum(
            "td,tk->dk", normed_low, grad_proj, preferred_element_type=jnp.float32
        )
        grad_normed = jnp.dot(grad_proj, proj_w.T, preferred_element_type=jnp.float32)
        grad_hidden_norm, term_gain_pre = pull_norm(grad_normed)
        grad_hidden = grad_result + grad_hidden_norm
        grad_proj_w = grad_proj_w + is_valid * term_proj_w
        grad_out_w = grad_out_w + is_valid * term_out_w
        grad_gain_pre = grad_gain_pre + is_valid * term_gain_pre
        grad_conv_weight = grad_conv_weight + is_valid * term_conv_weight
        grad_conv_bias = grad_conv_bias + is_valid * term_conv_bias
        grad_bias_dt = grad_bias_dt + is_valid * term_bias_dt
        grad_log_rate = grad_log_rate + is_valid * term_log_rate
        grad_skip_heads = grad_skip_heads + is_valid * term_skip
        grad_gain_gate = grad_gain_gate + is_valid * term_gain_gate
        grad_send = grad_hidden.astype(jnp.bfloat16)
        input_grads.append(
            jnp.where(section_index == 1, grad_send.astype(jnp.float32), grad_hidden)
        )
        received_back = from_behind(grad_send, "section", -1)
    stacked_grads = jnp.stack(input_grads)
    acts = jnp.stack(
        [
            lax.dynamic_index_in_dim(stacked_results, batch_index + section_index, keepdims=False)
            for batch_index in range(batches)
        ]
    )
    in_grad = jnp.stack(
        [
            lax.dynamic_index_in_dim(
                stacked_grads, batches - batch_index - section_index, keepdims=False
            )
            for batch_index in range(batches)
        ]
    )
    acts = acts.reshape(1, batches, 1, tokens_dev, D)
    in_grad = in_grad.reshape(1, batches, 1, tokens_dev, D)
    every_part = (
        lax.psum_scatter(
            grad_proj_w[None].astype(jnp.bfloat16), "wshard", scatter_dimension=1, tiled=True
        ).astype(jnp.float32),
        lax.psum_scatter(
            grad_out_w[None].astype(jnp.bfloat16), "wshard", scatter_dimension=1, tiled=True
        ).astype(jnp.float32),
        lax.psum_scatter(
            grad_gain_pre[None].astype(jnp.bfloat16), "wshard", scatter_dimension=1, tiled=True
        ).astype(jnp.float32),
        lax.psum_scatter(
            grad_conv_weight[None].astype(jnp.bfloat16), "wshard", scatter_dimension=2, tiled=True
        ).astype(jnp.float32),
        lax.psum_scatter(
            grad_conv_bias[None].astype(jnp.bfloat16), "wshard", scatter_dimension=1, tiled=True
        ).astype(jnp.float32),
        lax.psum_scatter(
            grad_bias_dt[None].astype(jnp.bfloat16), "wshard", scatter_dimension=1, tiled=True
        ).astype(jnp.float32),
        lax.psum_scatter(
            grad_log_rate[None].astype(jnp.bfloat16), "wshard", scatter_dimension=1, tiled=True
        ).astype(jnp.float32),
        lax.psum_scatter(
            grad_skip_heads[None].astype(jnp.bfloat16), "wshard", scatter_dimension=1, tiled=True
        ).astype(jnp.float32),
        lax.psum_scatter(
            grad_gain_gate[None].astype(jnp.bfloat16), "wshard", scatter_dimension=1, tiled=True
        ).astype(jnp.float32),
    )
    every_part = (
        lax.psum(every_part[0].astype(jnp.bfloat16), "seq").astype(jnp.float32),
        lax.psum(every_part[1].astype(jnp.bfloat16), "seq").astype(jnp.float32),
        lax.psum(every_part[2].astype(jnp.bfloat16), "seq").astype(jnp.float32),
        lax.psum(every_part[3].astype(jnp.bfloat16), "seq").astype(jnp.float32),
        lax.psum(every_part[4].astype(jnp.bfloat16), "seq").astype(jnp.float32),
        lax.psum(every_part[5].astype(jnp.bfloat16), "seq").astype(jnp.float32),
        lax.psum(every_part[6].astype(jnp.bfloat16), "seq").astype(jnp.float32),
        lax.psum(every_part[7].astype(jnp.bfloat16), "seq").astype(jnp.float32),
        lax.psum(every_part[8].astype(jnp.bfloat16), "seq").astype(jnp.float32),
    )
    part_in = every_part[0]
    part_out = every_part[1]
    small_parts = every_part[2:]
    return (
        acts,
        in_grad,
        small_parts[0],
        part_in,
        small_parts[1],
        small_parts[2],
        small_parts[3],
        small_parts[4],
        small_parts[5],
        small_parts[6],
        part_out,
    )


def solution(mesh):
    placed = (
        P(None, "wshard", "seq", None),
        P(None, "wshard", "seq", None),
        P(None, "wshard"),
        P("section", "wshard"),
        P("section", "wshard", None),
        P("section", None, "wshard"),
        P("section", "wshard"),
        P("section", "wshard"),
        P("section", "wshard"),
        P("section", "wshard"),
        P("section", "wshard"),
        P("section", "wshard", None),
    )
    return jax.shard_map(
        on_device,
        mesh=mesh,
        in_specs=placed,
        out_specs=(
            P("section", None, "wshard", "seq", None),
            P("section", None, "wshard", "seq", None),
            P("section", "wshard"),
            P("section", "wshard", None),
            P("section", None, "wshard"),
            P("section", "wshard"),
            P("section", "wshard"),
            P("section", "wshard"),
            P("section", "wshard"),
            P("section", "wshard"),
            P("section", "wshard", None),
        ),
        check_vma=False,
    )
```

profile of v0, /device:TPU:0, one launch (start us, length us, event | category | flops | bytes accessed | tf_op | source)
XLA Modules:
  0.0 1832.7 jit_solution(174978496468800826)
XLA Ops:
  35.6 90.0 %all-gather.21.cloned.1.call-done = bf16[1,1024,4384]{1,2,0:T(8,128)(2,1)} async-done(((bf16[1,512,4384]{1,2,0:T(8,128)(2,1)}), bf16[1,1024,4384]{1,2,0:T(8,128)(2,1)}) %all-gather.21.cloned.1.call-update) | async-done | bytes 8978448 | tf_op jit(solution)/shard_map/all_gather | solution.py:182
  166.1 19.4 %all-gather.9 = f32[8,1,32]{2,1,0:T(1,128)S(1)} all-gather(f32[1,1,32]{2,1,0:T(1,128)S(1)} %bitcast.1157), channel_id=1, replica_groups=mesh['section'=2,'seq'=8,'wshard'=2] {'seq'}, dimensions={0}, use_global_device_ids=true | all-gather | bytes 1152 | tf_op jit(solution)/shard_map/all_gather | solution.py:26
  189.8 92.1 %all-gather.25.cloned.1.call-done = f32[256,64,128]{2,1,0:T(8,128)} async-done(((f32[32,64,128]{2,1,0:T(8,128)}), f32[256,64,128]{2,1,0:T(8,128)}) %all-gather.25.cloned.1.call-update) | async-done | bytes 8388624 | tf_op jit(solution)/shard_map/all_gather | solution.py:26
  284.3 11.3 fusion.198
  299.3 39.1 %all-gather.23.cloned.1.call-done = bf16[1,2048,1024]{2,1,0:T(8,128)(2,1)} async-done(((bf16[1,1024,1024]{2,1,0:T(8,128)(2,1)}), bf16[1,2048,1024]{2,1,0:T(8,128)(2,1)}) %all-gather.23.cloned.1.call-update) | async-done | bytes 4194320 | tf_op jit(solution)/shard_map/all_gather | solution.py:183
  388.6 18.5 %all-gather.10 = f32[8,1,32]{2,1,0:T(1,128)S(1)} all-gather(f32[1,1,32]{2,1,0:T(1,128)} %bitcast.1159), channel_id=1, replica_groups=mesh['section'=2,'seq'=8,'wshard'=2] {'seq'}, dimensions={0}, use_global_device_ids=true | all-gather | bytes 1152 | tf_op jit(solution)/shard_map/all_gather | solution.py:26
  411.4 100.6 %all-gather.27.cloned.1.call-done = f32[256,64,128]{2,1,0:T(8,128)} async-done(((f32[32,64,128]{2,1,0:T(8,128)}), f32[256,64,128]{2,1,0:T(8,128)}) %all-gather.27.cloned.1.call-update) | async-done | bytes 8388624 | tf_op jit(solution)/shard_map/all_gather | solution.py:26
  515.3 11.3 fusion.200
  568.4 15.8 fusion.196
  589.2 25.9 %all-gather.11 = f32[8,1,32]{2,1,0:T(1,128)S(1)} all-gather(f32[1,1,32]{2,1,0:T(1,128)S(1)} %bitcast.1158), channel_id=1, replica_groups=mesh['section'=2,'seq'=8,'wshard'=2] {'seq'}, dimensions={0}, use_global_device_ids=true | all-gather | bytes 1152 | tf_op jit(solution)/shard_map/all_gather | solution.py:26
  618.7 10.9 fusion.54
  629.6 92.2 %all-gather.29.cloned.1.call-done = f32[256,64,128]{2,1,0:T(8,128)} async-done(((f32[32,64,128]{2,1,0:T(8,128)}), f32[256,64,128]{2,1,0:T(8,128)}) %all-gather.29.cloned.1.call-update) | async-done | bytes 8388624 | tf_op jit(solution)/shard_map/all_gather | solution.py:26
  742.2 28.0 %all-gather.3 = bf16[8,1,32]{2,1,0:T(2,128)(2,1)S(1)} all-gather(bf16[1,1,32]{2,1,0:T(2,128)(2,1)S(1)} %copy.317), channel_id=5, replica_groups=mesh['section'=2,'seq'=8,'wshard'=2] {'seq'}, dimensions={0}, use_global_device_ids=true | all-gather | bytes 576 | tf_op jit(solution)/shard_map/all_gather | solution.py:42
  774.7 48.6 %all-gather.31.cloned.1.call-done = bf16[256,64,128]{2,1,0:T(8,128)(2,1)} async-done(((bf16[32,64,128]{2,1,0:T(8,128)(2,1)}), bf16[256,64,128]{2,1,0:T(8,128)(2,1)}) %all-gather.31.cloned.1.call-update) | async-done | bytes 4194320 | tf_op jit(solution)/shard_map/all_gather | solution.py:42
  850.0 12.7 fusion.80
  977.4 16.4 all-gather.5
  1005.1 42.3 %all-gather.33.cloned.1.call-done = bf16[256,64,128]{2,1,0:T(8,128)(2,1)} async-done(((bf16[32,64,128]{2,1,0:T(8,128)(2,1)}), bf16[256,64,128]{2,1,0:T(8,128)(2,1)}) %all-gather.33.cloned.1.call-update) | async-done | bytes 4194320 | tf_op jit(solution)/shard_map/all_gather | solution.py:42
  1072.9 12.7 fusion.82
  1156.5 11.4 fusion.34
  1218.8 18.9 %all-gather.7 = bf16[8,1,32]{2,1,0:T(2,128)(2,1)S(1)} all-gather(bf16[1,1,32]{2,1,0:T(2,128)(2,1)S(1)} %copy.367), channel_id=9, replica_groups=mesh['section'=2,'seq'=8,'wshard'=2] {'seq'}, dimensions={0}, use_global_device_ids=true | all-gather | bytes 576 | tf_op jit(solution)/shard_map/all_gather | solution.py:42
  1258.0 12.1 all-gather.35.cloned.1.call-done
  1270.3 14.2 while.59
  1296.2 11.1 multiply_reduce_fusion.12
  1307.7 13.8 fusion.84
  1365.3 17.2 fusion.78
  1403.2 84.6 %reduce-scatter.24.cloned.1.call-done = bf16[1,512,4384]{1,2,0:T(8,128)(2,1)} async-done(((bf16[1,1024,4384]{1,2,0:T(8,128)(2,1)}), bf16[1,512,4384]{1,2,0:T(8,128)(2,1)}) %reduce-scatter.24.cloned.1.call-update) | async-done | bytes 4489232 | tf_op jit(solution)/shard_map/reduce_scatter | solution.py:383
  1517.7 11.4 reduce-scatter.34.cloned.1.call-done
  1529.9 11.1 reduce-scatter.36.cloned.1.call-done
  1541.7 16.7 reduce-scatter.32.cloned.1.call-done
  1573.2 16.4 reduce-scatter.30.cloned.1.call-done
  1591.4 39.1 %all-reduce.52 = (bf16[1,512]{1,0:T(2,128)(2,1)S(1)}, bf16[1,4,1152]{2,1,0:T(4,128)(2,1)S(1)}, bf16[1,1152]{1,0:T(2,128)(2,1)S(1)}, bf16[1,16]{1,0:T(2,128)(2,1)...) all-reduce(bf16[1,512]{1,0:T(2,128)(2,1)S(1)} %copy.479, ...), channel_id=1, replica_groups=mesh['section'=2,'seq'=8,'wshard'=2] {'seq'}, use_global_device_ids=true, to_apply=%region_85.87 | all-reduce | flops 7344 | bytes 29376 | tf_op jit(solution)/shard_map/psum | solution.py:414
  1634.4 181.5 %all-reduce.56.cloned.1.call-done = (bf16[1,512,4384]{1,2,0:T(8,128)(2,1)}, bf16[1,1024,1024]{2,1,0:T(8,128)(2,1)}) async-done(((bf16[1,512,4384]{1,2,0:T(8,128)(2,1)}, bf16[1,1024,1024]{2,1,0:T(8,128)(2,1)}), (bf16[1,512,4384]{1,2,0:T(8,128)(2,1)}, bf16[1,1024,1024]{2,1,0:T(8,128)(2,1)})) %all-reduce.56.cloned.1.call-update) | async-done | bytes 6586384 | tf_op jit(solution)/shard_map/psum | solution.py:412
  (1202 shorter events, 695.5 us)
Async XLA Ops:
  7.3 118.3 %all-gather.21.cloned.1.call-start = ((), (), s32[]{:S(2)}) async-start(), calls=%async_computation.9 | async-start | bytes 13467648 | tf_op jit(solution)/shard_map/all_gather | solution.py:182
  8.0 273.9 %all-gather.25.cloned.1.call-start = ((), (), s32[]{:S(2)}) async-start(), calls=%async_computation.13 | async-start | bytes 9437184 | tf_op jit(solution)/shard_map/all_gather | solution.py:26
  16.0 116.4 %copy-start.236 = (f32[32]{0:T(128)}, f32[32]{0:T(128)S(1)}, u32[]{:S(2)}) copy-start(f32[32]{0:T(128)S(1)} %get-tuple-element.1333) | copy-start | bytes 388
  16.0 116.4 %copy-start.241 = (f32[32]{0:T(128)}, f32[32]{0:T(128)S(1)}, u32[]{:S(2)}) copy-start(f32[32]{0:T(128)S(1)} %exp.239) | copy-start | bytes 388
  17.9 147.4 %copy-start.196 = (f32[256]{0:T(256)}, f32[256]{0:T(256)S(1)}, u32[]{:S(2)}) copy-start(f32[256]{0:T(256)S(1)} %fusion.660) | copy-start | bytes 3076
  34.0 110.0 %copy-start.224 = (f32[256]{0:T(256)}, f32[256]{0:T(256)S(1)}, u32[]{:S(2)}) copy-start(f32[256]{0:T(256)S(1)} %get-tuple-element.1482) | copy-start | bytes 3076
  135.6 6.9 collective-permute-start
  157.7 180.7 %all-gather.23.cloned.1.call-start = ((), (), s32[]{:S(2)}) async-start(), calls=%async_computation.10 | async-start | bytes 6291456 | tf_op jit(solution)/shard_map/all_gather | solution.py:183
  158.4 353.5 %all-gather.27.cloned.1.call-start = ((), (), s32[]{:S(2)}) async-start(), calls=%async_computation.14 | async-start | bytes 9437184 | tf_op jit(solution)/shard_map/all_gather | solution.py:26
  342.6 10.4 collective-permute-start.1
  363.9 8.6 collective-permute-start.2
  387.8 334.0 %all-gather.29.cloned.1.call-start = ((), (), s32[]{:S(2)}) async-start(), calls=%async_computation.15 | async-start | bytes 9437184 | tf_op jit(solution)/shard_map/all_gather | solution.py:26
  531.8 4.9 collective-permute-start.3
  553.6 10.7 collective-permute-start.4
  589.0 234.3 %all-gather.31.cloned.1.call-start = ((), (), s32[]{:S(2)}) async-start(), calls=%async_computation.16 | async-start | bytes 4718592 | tf_op jit(solution)/shard_map/all_gather | solution.py:42
  741.3 306.1 %all-gather.33.cloned.1.call-start = ((), (), s32[]{:S(2)}) async-start(), calls=%async_computation.17 | async-start | bytes 4718592 | tf_op jit(solution)/shard_map/all_gather | solution.py:42
  906.4 5.9 collective-permute-start.5
  950.8 13.9 collective-permute-start.6
  975.8 294.4 %all-gather.35.cloned.1.call-start = ((), (), s32[]{:S(2)}) async-start(), calls=%async_computation.18 | async-start | bytes 4718592 | tf_op jit(solution)/shard_map/all_gather | solution.py:42
  1155.1 16.3 collective-permute-start.7
  1184.5 4.1 collective-permute-start.8
  1197.3 205.9 %reduce-scatter.26.cloned.1.call-start = ((), (), s32[]{:S(2)}) async-start(), calls=%async_computation.12 | async-start | bytes 6291456 | tf_op jit(solution)/shard_map/reduce_scatter | solution.py:386
  1258.0 229.8 %reduce-scatter.24.cloned.1.call-start = ((), (), s32[]{:S(2)}) async-start(), calls=%async_computation.11 | async-start | bytes 13467648 | tf_op jit(solution)/shard_map/reduce_scatter | solution.py:383
  1349.2 10.3 collective-permute-start.9
  1382.8 128.6 %reduce-scatter.38.cloned.1.call-start = ((), (), s32[]{:S(2)}) async-start(), calls=%async_computation.24 | async-start | bytes 12288
  1384.7 131.9 %reduce-scatter.40.cloned.1.call-start = ((), (), s32[]{:S(2)}) async-start(), calls=%async_computation.25 | async-start | bytes 786432
  1386.0 143.1 %reduce-scatter.34.cloned.1.call-start = ((), (), s32[]{:S(2)}) async-start(), calls=%async_computation.22 | async-start | bytes 12288
  1388.1 152.8 %reduce-scatter.36.cloned.1.call-start = ((), (), s32[]{:S(2)}) async-start(), calls=%async_computation.23 | async-start | bytes 12288
  1388.9 169.4 %reduce-scatter.32.cloned.1.call-start = ((), (), s32[]{:S(2)}) async-start(), calls=%async_computation.21 | async-start | bytes 884736
  1389.5 182.7 %reduce-scatter.28.cloned.1.call-start = ((), (), s32[]{:S(2)}) async-start(), calls=%async_computation.19 | async-start | bytes 393216
  1398.1 191.5 %reduce-scatter.30.cloned.1.call-start = ((), (), s32[]{:S(2)}) async-start(), calls=%async_computation.20 | async-start | bytes 884736
  1402.7 413.1 %all-reduce.56.cloned.1.call-start = ((), (), s32[]{:S(2)}) async-start(), calls=%async_computation.26 | async-start | bytes 13172736 | tf_op jit(solution)/shard_map/psum | solution.py:412
  (335 other events, 2574.0 us)
Sparse Core Ops, SparseCore 0:
  9.7 115.8 all-gather.20
  157.8 124.0 all-gather.24
  283.4 54.9 all-gather.22
  387.9 124.0 all-gather.26
  589.2 132.5 all-gather.28
  741.4 81.8 all-gather.30
  975.9 71.4 all-gather.32
  1197.4 72.7 all-gather.34
  1273.0 52.5 reduce-scatter.25
  1382.9 104.8 reduce-scatter.23
  1490.1 9.7 reduce-scatter.37
  1502.0 14.5 reduce-scatter.39
  1519.4 9.7 reduce-scatter.33
  1531.1 9.7 reduce-scatter.35
  1543.0 15.2 reduce-scatter.31
  1560.5 11.6 reduce-scatter.27
  1574.3 15.2 reduce-scatter.29
  1594.1 221.7 all-reduce.55
where the time goes:
time: 1840 us; the launch traced here: 1830 us
  waiting for transfers between devices  857 us (47%)
  matrix products  367 us (20%)
  other arithmetic  261 us (14%)
  blocking collectives  190 us (10%)
  local copies, waits for them, and re-layouts  109 us (6%)
  starting transfers between devices  23.9 us (1%)
  between operations  22.2 us (1%)
    all_gather x3, waiting for transfers between devices, carried_in(): gathered = jax.tree.map(lambda a: lax.all_gather(a, axis), part)  285 us
    psum x1, waiting for transfers between devices, on_device(): lax.psum(every_part[0].astype(jnp.bfloat16), 'seq').astype(jnp.float32)  181 us
    dot_general x12, matrix products, group_step(): jnp.einsum('tsh,shp->thp', decays * scores[:, :, None], scaled_x, precisi...  136 us
    all_gather x3, waiting for transfers between devices, entering_2(): lax.all_gather(a.astype(kind), axis)  103 us
    all_gather x1, waiting for transfers between devices, on_device(): lax.all_gather(w_in, 'wshard', axis=1, tiled=True)  90 us
    reduce_scatter x1, waiting for transfers between devices, on_device(): lax.psum_scatter(grad_proj_w[None].astype(jnp.bfloat16), 'wshard', scatte...  84.6 us
    unnamed x25, waiting for transfers between devices  69.7 us
    all_gather x3, blocking collectives, carried_in(): gathered = jax.tree.map(lambda a: lax.all_gather(a, axis), part)  63.9 us
  transfers between devices with their start and end apart: 28, of which 18 were waited for; matrix products, arithmetic and copies ran while one was open for 18% of the time, Pallas kernels for 0%

commit v1 on v0

v1 whole, which is shorter than its diff:
```python
import jax
import jax.numpy as jnp
from jax import lax
from jax.experimental import pallas as pl
from jax.experimental.pallas import tpu as pltpu
from jax.sharding import PartitionSpec as P

D = 1024
DI = 2048
H = 32
HEAD = DI // H
N = 128
K = 4
DCONV = 2304
DCD = DCONV + H
PAIR = 2 * HEAD
WIDE = 512
BLOCK = 256
EDGE = 8
MESSAGE = DI + 128
EPSILON = 1e-05
LOG2E = 1.4426950408889634
FAR = -1e30
F32 = jnp.float32
BF16 = jnp.bfloat16
HIGH = lax.Precision.HIGHEST


def dot(a, b):
    return jnp.dot(a, b, preferred_element_type=F32)


def dot_nt(a, b):
    return lax.dot_general(a, b, (((1,), (1,)), ((), ())), preferred_element_type=F32)


def dot_tn(a, b):
    return lax.dot_general(a, b, (((0,), (0,)), ((), ())), preferred_element_type=F32)


def iota(shape, dim):
    return lax.broadcasted_iota(jnp.int32, shape, dim)


def ones_where(condition):
    return jnp.where(condition, 1.0, 0.0).astype(F32)


def two_parts(values):
    high = values.astype(BF16)
    return high, (values - high.astype(F32)).astype(BF16)


def spread(values, start, width):
    pick = ones_where((start + iota((H, width), 1)) // HEAD == iota((H, width), 0)).astype(BF16)
    high, low = two_parts(values)
    return dot(high, pick) + dot(low, pick)


def head_sums(values, start):
    width = values.shape[1]
    pick = ones_where((start + iota((width, H), 0)) // HEAD == iota((width, H), 1)).astype(BF16)
    high, low = two_parts(values)
    return dot(high, pick) + dot(low, pick)


def sigmoid(values):
    return 0.5 * jnp.tanh(0.5 * values) + 0.5


def rows_of_one(row):
    return jnp.broadcast_to(row, (EDGE, row.shape[1]))


def segments(place, rows):
    offset, bound = place[0], place[1]
    position = offset + iota((rows, 1), 0)
    segment = ones_where(position >= bound)
    before = jnp.where(offset - 1 >= bound, 1.0, 0.0).astype(F32)
    last = jnp.where(offset + rows - 1 >= bound, 1.0, 0.0).astype(F32)
    return position, segment, before, last


def tap_masks(place, position):
    bound = place[1]
    return [
        ones_where((position - back >= bound) == (position >= bound)) if back else None
        for back in range(K)
    ]


def decay_lanes(through):
    high, low = two_parts(jnp.broadcast_to(through, (N, H)))
    first = ones_where(iota((H, 128), 0) == iota((H, 128), 1)).astype(BF16)
    second = ones_where(iota((H, 128), 0) + H == iota((H, 128), 1)).astype(BF16)
    return (dot(high, first) + dot(low, second)).astype(BF16)


def states_kernel(place, cd, edge, conv_w, conv_b, dt_bias, a_log, pre, act, step, cum, message):
    rows = cd.shape[0]
    position, segment, before, last = segments(place, rows)
    masks = tap_masks(place, position)
    step_now = jax.nn.softplus(cd[:, DCONV:] + dt_bias[...])
    log_decay = -step_now * jnp.exp(a_log[...])
    lower = ones_where(iota((rows, rows), 0) >= iota((rows, rows), 1))
    summed = jnp.dot(lower, log_decay, precision=HIGH, preferred_element_type=F32)
    step[...] = step_now
    cum[...] = summed
    total = summed[rows - 1 :, :]
    weight = step_now * jnp.where(segment == last, jnp.exp(total - summed), 0.0)
    for start in range(0, DCONV, BLOCK):
        here = slice(start, start + BLOCK)
        values = cd[:, here]
        extended = jnp.concatenate([edge[:, here], values], axis=0)
        conv = conv_b[:, here] + conv_w[K - 1 : K, here] * values
        for back in range(1, K):
            moved = pltpu.roll(extended, back, 0)[EDGE:]
            conv = conv + conv_w[K - 1 - back : K - back, here] * moved * masks[back]
        pre[:, here] = conv
        act[:, here] = conv * sigmoid(conv)
    in_t = jnp.transpose(act[:, DI : DI + N]).astype(BF16)
    for start in range(0, DI, WIDE):
        here = slice(start, start + WIDE)
        scaled = act[:, here] * spread(weight, start, WIDE)
        message[:, here] = dot(in_t, scaled.astype(BF16)).astype(BF16)
    through = jnp.exp(total) * jnp.where(before == last, 1.0, 0.0)
    message[:, DI:] = decay_lanes(through)


def carry_kernel(reverse, gathered, out, *scratch):
    count, rows = gathered.shape[0], gathered.shape[1]
    pick = ones_where(iota((2 * H, DI), 1) // HEAD == iota((2 * H, DI), 0) % H).astype(BF16)
    state = jnp.zeros((rows, DI), F32)
    for source in range(count - 1, -1, -1) if reverse else range(count):
        out[source] = state.astype(BF16)
        part = gathered[source]
        state = dot(part[:, DI : DI + 2 * H], pick) * state + part[:, :DI].astype(F32)


def intra_kernel(place, act, step, cum, skip, local):
    rows = act.shape[0]
    position, segment, _, _ = segments(place, rows)
    in_b = act[:, DI : DI + N].astype(BF16)
    out_c = act[:, DI + N :].astype(BF16)
    scores = dot_nt(out_c, in_b)
    across = place[0] + iota((1, rows), 1)
    same = segment == ones_where(across >= place[1])
    bias = jnp.where((position >= across) & same, 0.0, FAR)
    level = cum[...] * LOG2E
    level_t = jnp.transpose(level)
    steps = step[...]
    skips = rows_of_one(skip[...])
    left = iota((rows, PAIR), 1) < HEAD
    for pair in range(H // 2):
        start = pair * PAIR
        here = slice(start, start + PAIR)
        values = act[:, here]
        scaled = (values * spread(steps, start, PAIR)).astype(BF16)
        outs = []
        for head in (2 * pair, 2 * pair + 1):
            decay = jnp.exp2(level[:, head : head + 1] - level_t[head : head + 1, :] + bias)
            outs.append(dot((decay * scores).astype(BF16), scaled))
        local[:, here] = jnp.where(left, outs[0], outs[1]) + spread(skips, start, PAIR)[:1] * values


def gate_kernel(place, entry, local, act, cum, gate, gain, mixed, gated, kept):
    rows = act.shape[0]
    _, segment, before, _ = segments(place, rows)
    enter = jnp.exp(cum[...]) * ones_where(segment == before)
    out_c = act[:, DI + N :].astype(BF16)
    square = jnp.zeros((rows, 1), F32)
    for start in range(0, DI, WIDE):
        here = slice(start, start + WIDE)
        y = local[:, here] + dot(out_c, entry[:, here]) * spread(enter, start, WIDE)
        mixed[:, here] = y
        raw = gate[:, here]
        u = y * raw * sigmoid(raw)
        kept[:, here] = u
        square = square + jnp.sum(u * u, axis=1, keepdims=True)
    scale = lax.rsqrt(square / DI + EPSILON)
    for start in range(0, DI, WIDE):
        here = slice(start, start + WIDE)
        gated[:, here] = (kept[:, here] * scale * gain[:, here]).astype(BF16)


def gate_back_kernel(
    place, grad_gated, mixed, gate, gain, cum, act, grad_mixed, grad_gate, grad_gain, message, kept
):
    rows = act.shape[0]
    _, segment, before, last = segments(place, rows)
    summed = cum[...]
    enter = jnp.exp(summed) * ones_where(segment == before)
    out_t = jnp.transpose(act[:, DI + N :]).astype(BF16)
    square = jnp.zeros((rows, 1), F32)
    cross = jnp.zeros((rows, 1), F32)
    for start in range(0, DI, WIDE):
        here = slice(start, start + WIDE)
        raw = gate[:, here]
        u = mixed[:, here] * raw * sigmoid(raw)
        kept[:, here] = u
        square = square + jnp.sum(u * u, axis=1, keepdims=True)
        cross = cross + jnp.sum(grad_gated[:, here] * gain[:, here] * u, axis=1, keepdims=True)
    scale = lax.rsqrt(square / DI + EPSILON)
    pulled = scale * scale * scale * cross / DI
    for start in range(0, DI, WIDE):
        here = slice(start, start + WIDE)
        raw = gate[:, here]
        u = kept[:, here]
        up = grad_gated[:, here]
        grad_gain[:, here] = jnp.sum(up * u * scale, axis=0, keepdims=True)
        grad_u = scale * up * gain[:, here] - pulled * u
        curve = sigmoid(raw)
        grad_y = grad_u * raw * curve
        grad_gate[:, here] = (
            grad_u * mixed[:, here] * curve * (1.0 + raw * (1.0 - curve))
        ).astype(BF16)
        grad_mixed[:, here] = grad_y
        pull = (grad_y * spread(enter, start, WIDE)).astype(BF16)
        message[:, here] = dot(out_t, pull).astype(BF16)
    through = jnp.exp(summed[rows - 1 :, :]) * jnp.where(before == last, 1.0, 0.0)
    message[:, DI:] = decay_lanes(through)


def intra_back_kernel(
    place, act, step, cum, grad_mixed, entry, grad_scaled, grad_bc, grad_cum, grad_scores, across_sum
):
    rows = act.shape[0]
    position, segment, before, _ = segments(place, rows)
    in_b = act[:, DI : DI + N].astype(BF16)
    out_c = act[:, DI + N :].astype(BF16)
    scores = dot_nt(in_b, out_c)
    across = place[0] + iota((1, rows), 1)
    same = segment == ones_where(across >= place[1])
    bias = jnp.where((across >= position) & same, 0.0, FAR)
    summed = cum[...]
    level = summed * LOG2E
    level_t = jnp.transpose(level)
    steps = step[...]
    left = iota((rows, PAIR), 1) < HEAD
    lane = iota((rows, H), 1)
    grad_scores[...] = jnp.zeros((rows, rows), F32)
    down_sum = jnp.zeros((rows, H), F32)
    for pair in range(H // 2):
        start = pair * PAIR
        here = slice(start, start + PAIR)
        scaled = act[:, here] * spread(steps, start, PAIR)
        up = grad_mixed[:, here].astype(BF16)
        outs = []
        for head in (2 * pair, 2 * pair + 1):
            mine = left if head % 2 == 0 else jnp.logical_not(left)
            grad_weight = dot_nt(jnp.where(mine, scaled, 0.0).astype(BF16), up)
            decay = jnp.exp2(level_t[head : head + 1, :] - level[:, head : head + 1] + bias)
            weight = decay * scores
            grad_scores[...] += decay * grad_weight
            flow = weight * grad_weight
            across_sum[head : head + 1, :] = jnp.sum(flow, axis=0, keepdims=True)
            down_sum = down_sum + jnp.where(lane == head, jnp.sum(flow, axis=1, keepdims=True), 0.0)
            outs.append(dot(weight.astype(BF16), up))
        grad_scaled[:, here] = jnp.where(left, outs[0], outs[1])
    enter = jnp.exp(summed) * ones_where(segment == before)
    grad_out = jnp.zeros((rows, N), F32)
    grad_enter = jnp.zeros((rows, H), F32)
    for start in range(0, DI, WIDE):
        here = slice(start, start + WIDE)
        entered = entry[:, here]
        pull = grad_mixed[:, here] * spread(enter, start, WIDE)
        grad_out = grad_out + dot_nt(pull.astype(BF16), entered)
        grad_enter = grad_enter + head_sums(pull * dot(out_c, entered), start)
    low = grad_scores[...].astype(BF16)
    grad_bc[:, :N] = dot(low, out_c)
    grad_bc[:, N:] = grad_out + dot(jnp.transpose(grad_scores[...]).astype(BF16), in_b)
    grad_cum[...] = jnp.transpose(across_sum[...]) - down_sum + grad_enter


def finish_kernel(
    place,
    cd,
    edge,
    pre,
    act,
    step,
    cum,
    grad_mixed,
    grad_scaled,
    grad_bc,
    grad_cum,
    entry,
    leaving,
    conv_w,
    dt_bias,
    a_log,
    skip,
    grad_cd,
    grad_tail,
    grad_edge,
    grad_conv_w,
    grad_conv_b,
    grad_heads,
    grad_pre,
):
    rows = cd.shape[0]
    position, segment, before, last = segments(place, rows)
    masks = tap_masks(place, position)
    summed = cum[...]
    total = summed[rows - 1 :, :]
    to_end = jnp.where(segment == last, jnp.exp(total - summed), 0.0)
    steps = step[...]
    skips = rows_of_one(skip[...])
    in_b = act[:, DI : DI + N].astype(BF16)

    def silu_slope(values):
        curve = sigmoid(values)
        return curve * (1.0 + values * (1.0 - curve))

    grad_end = jnp.zeros((rows, H), F32)
    grad_step = jnp.zeros((rows, H), F32)
    grad_in = grad_bc[:, :N]
    grad_through = jnp.zeros((EDGE, H), F32)
    grad_skip = jnp.zeros((EDGE, H), F32)
    for start in range(0, DI, WIDE):
        here = slice(start, start + WIDE)
        values = act[:, here]
        up = grad_mixed[:, here]
        left = leaving[:, here]
        step_wide = spread(steps, start, WIDE)
        end_wide = spread(to_end, start, WIDE)
        pulled = dot(in_b, left) * end_wide
        scaled = values * step_wide
        grad_now = grad_scaled[:, here] + pulled
        grad_end = grad_end + head_sums(scaled * pulled, start)
        grad_step = grad_step + head_sums(grad_now * values, start)
        grad_in = grad_in + dot_nt((end_wide * scaled).astype(BF16), left)
        states = jnp.sum(entry[:, here].astype(F32) * left.astype(F32), axis=0, keepdims=True)
        grad_through = grad_through + head_sums(rows_of_one(states), start)
        skipped = jnp.sum(up * values, axis=0, keepdims=True)
        grad_skip = grad_skip + head_sums(rows_of_one(skipped), start)
        grad_x = grad_now * step_wide + spread(skips, start, WIDE)[:1] * up
        grad_pre[:, here] = grad_x * silu_slope(pre[:, here])
    grad_pre[:, DI : DI + N] = grad_in * silu_slope(pre[:, DI : DI + N])
    grad_pre[:, DI + N :] = grad_bc[:, N:] * silu_slope(pre[:, DI + N :])
    through = jnp.exp(total) * jnp.where(before == last, 1.0, 0.0)
    at_last = jnp.sum(grad_end, axis=0, keepdims=True) + through * grad_through[:1]
    upper = ones_where(iota((rows, rows), 1) >= iota((rows, rows), 0))
    grad_log = at_last + jnp.dot(
        upper, grad_cum[...] - grad_end, precision=HIGH, preferred_element_type=F32
    )
    rate = jnp.exp(a_log[...])
    grad_step = grad_step - rate * grad_log
    grad_raw = grad_step * sigmoid(cd[:, DCONV:] + dt_bias[...])
    grad_cd[:, DCONV:] = grad_raw.astype(BF16)
    grad_heads[0:1, :] = jnp.sum(grad_raw, axis=0, keepdims=True)
    grad_heads[1:2, :] = jnp.sum(grad_log * -steps * rate, axis=0, keepdims=True)
    grad_heads[2:3, :] = grad_skip[:1]
    grad_heads[3:, :] = jnp.zeros((EDGE - 3, H), F32)
    nothing = jnp.zeros((EDGE, BLOCK), F32)
    for start in range(0, DCONV, BLOCK):
        here = slice(start, start + BLOCK)
        values = cd[:, here]
        extended = jnp.concatenate([edge[:, here], values], axis=0)
        up = grad_pre[:, here]
        grad_conv_b[:, here] = jnp.sum(up, axis=0, keepdims=True)
        grad_conv_w[K - 1 : K, here] = jnp.sum(up * values, axis=0, keepdims=True)
        spilled = nothing
        grad_in_now = conv_w[K - 1 : K, here] * up
        for back in range(1, K):
            moved = pltpu.roll(extended, back, 0)[EDGE:]
            masked = up * masks[back]
            grad_conv_w[K - 1 - back : K - back, here] = jnp.sum(
                masked * moved, axis=0, keepdims=True
            )
            framed = jnp.concatenate([nothing, masked, nothing], axis=0)
            returned = pltpu.roll(framed, rows + 2 * EDGE - back, 0)
            tap = conv_w[K - 1 - back : K - back, here]
            spilled = spilled + tap * returned[:EDGE]
            grad_in_now = grad_in_now + tap * returned[EDGE : EDGE + rows]
        grad_edge[:, here] = spilled
        grad_tail[:, here] = grad_in_now[rows - EDGE :]
        grad_cd[:, here] = grad_in_now.astype(BF16)


def call(body, outs, scratch, *operands):
    whole = pl.BlockSpec(memory_space=pltpu.VMEM)
    scalars = [pl.BlockSpec(memory_space=pltpu.SMEM)] if operands[0].dtype == jnp.int32 else []
    return pl.pallas_call(
        body,
        out_shape=[jax.ShapeDtypeStruct(shape, kind) for shape, kind in outs],
        in_specs=scalars + [whole] * (len(operands) - len(scalars)),
        out_specs=[whole] * len(outs),
        scratch_shapes=[pltpu.VMEM(shape, kind) for shape, kind in scratch],
        compiler_params=pltpu.CompilerParams(vmem_limit_bytes=56 * 1024 * 1024),
    )(*operands)


def turned(block, axis, distance):
    count = lax.axis_size(axis)
    return lax.ppermute(block, axis, [(i, (i + distance) % count) for i in range(count)])


def from_behind(block, axis, distance):
    devices = range(lax.axis_size(axis))
    route = [(i - distance, i) for i in devices if i - distance in devices]
    return lax.ppermute(block, axis, route)


def exchange_states(message, reverse):
    count = lax.axis_size("seq")
    rows = N // count
    sent = message.reshape(count, rows, MESSAGE)
    gathered = lax.all_to_all(sent, "seq", 0, 0)

    def body(gathered_ref, out_ref):
        carry_kernel(reverse, gathered_ref, out_ref)

    (states,) = call(body, [((count, rows, DI), BF16)], [], gathered)
    return lax.all_to_all(states, "seq", 0, 0).reshape(N, DI)


def on_device(
    inputs,
    cotangent,
    boundary,
    norm_gain,
    w_in,
    conv_w,
    conv_b,
    dt_bias,
    a_log,
    skip_gain,
    gate_norm,
    w_out,
):
    section = lax.axis_index("section")
    sections = lax.axis_size("section")
    shard = lax.axis_index("wshard")
    shards = lax.axis_size("wshard")
    batches, _, rows, _ = inputs.shape
    offset = lax.axis_index("seq") * rows

    source = lax.dynamic_index_in_dim(inputs[:, 0], section, keepdims=False)
    upstream = lax.dynamic_index_in_dim(cotangent[:, 0], section, keepdims=False)
    bound = lax.dynamic_index_in_dim(boundary[:, 0], section, keepdims=False)
    place = jnp.stack([offset, bound]).astype(jnp.int32)

    small_parts = (norm_gain, conv_w, conv_b, dt_bias, a_log, skip_gain, gate_norm)
    flat = jnp.concatenate([part.reshape(-1) for part in small_parts])
    every_small = lax.all_gather(flat, ("section", "wshard")).reshape(sections, shards, -1)

    def small_of(layer):
        out, at = [], 0
        for part in small_parts:
            size = part.size
            piece = every_small[layer, :, at : at + size]
            at += size
            piece = piece.reshape((shards,) + part.shape[1:])
            if part.ndim == 3:
                out.append(jnp.moveaxis(piece, 0, 1).reshape(part.shape[1], -1))
            else:
                out.append(piece.reshape(1, -1))
        return out

    own_blocks = (w_in[0, :, DI:], w_in[0, :, :DI], w_out[0])
    block_at = [(shard + away) % shards for away in range(shards)]
    weights = [[], []]
    for own in own_blocks:
        blocks = [own] + [turned(own, "wshard", -away) for away in range(1, shards)]
        others = [turned(block, "section", 1) for block in blocks]
        for layer in range(sections):
            weights[layer].append(
                [jnp.where(section == layer, a, b) for a, b in zip(blocks, others)]
            )

    def times(low, blocks):
        total = None
        for at, block in zip(block_at, blocks):
            size = block.shape[0]
            part = lax.dynamic_slice_in_dim(low, at * size, size, 1)
            term = jnp.dot(part, block, preferred_element_type=F32)
            total = term if total is None else total + term
        return total

    def times_back(terms, blocks):
        size = blocks[0].shape[0]
        parts = []
        for columns in range(shards):
            parts.append(
                sum(
                    lax.dot_general(
                        low, blocks_now[columns], (((1,), (1,)), ((), ())), preferred_element_type=F32
                    )
                    for low, blocks_now in terms
                )
            )
        if shards == 2:
            return jnp.where(
                shard == 0,
                jnp.concatenate(parts, axis=1),
                jnp.concatenate(parts[::-1], axis=1),
            )
        out = jnp.zeros((rows, size * shards), F32)
        for at, part in zip(block_at, parts):
            out = lax.dynamic_update_slice_in_dim(out, part, at * size, 1)
        return out

    def layer_forward(layer, hidden_low):
        w_cd, w_gate, w_last = weights[layer]
        gain_pre, taps, conv_bias, bias_dt, log_rate, skip, gain_gate = small_of(layer)
        hidden = hidden_low.astype(F32)
        scale = lax.rsqrt(jnp.mean(hidden * hidden, axis=-1, keepdims=True) + EPSILON)
        normed_low = (hidden * scale * gain_pre).astype(BF16)
        cd = times(normed_low, w_cd)
        edge = from_behind(cd[rows - EDGE :, :DCONV], "seq", 1)
        gate = times(normed_low, w_gate)
        pre, act, step, cum, message = call(
            states_kernel,
            [
                ((rows, DCONV), F32),
                ((rows, DCONV), F32),
                ((rows, H), F32),
                ((rows, H), F32),
                ((N, MESSAGE), BF16),
            ],
            [],
            place,
            cd,
            edge,
            taps,
            conv_bias,
            bias_dt,
            log_rate,
        )
        entry = exchange_states(message, False)
        (local,) = call(intra_kernel, [((rows, DI), F32)], [], place, act, step, cum, skip)
        mixed, gated_low = call(
            gate_kernel,
            [((rows, DI), F32), ((rows, DI), BF16)],
            [((rows, DI), F32)],
            place,
            entry,
            local,
            act,
            cum,
            gate,
            gain_gate,
        )
        result = (hidden + times(gated_low, w_last)).astype(BF16)
        kept = (hidden, scale, normed_low, cd, edge, gate, pre, act, step, cum, entry, mixed, gated_low)
        return result, kept

    def weight_terms(low, up):
        size = low.shape[1] // shards
        half = size // sections
        out = []
        for turn in range(sections):
            which = (section + turn) % sections
            out.append(
                [
                    lax.dot_general(
                        lax.dynamic_slice_in_dim(low, at * size + which * half, half, 1),
                        up,
                        (((0,), (0,)), ((), ())),
                        preferred_element_type=F32,
                    )
                    for at in block_at
                ]
            )
        return out

    def reduce_weight(low, up):
        terms = weight_terms(low, up)
        own = terms[0]
        for turn in range(1, sections):
            sent = [turned(block.astype(BF16), "section", turn) for block in terms[turn]]
            own = [a + b.astype(F32) for a, b in zip(own, sent)]
        total = own[0]
        for away in range(1, shards):
            total = total + turned(own[away].astype(BF16), "wshard", away).astype(F32)
        return lax.psum(total.astype(BF16), "seq")

    def layer_backward(layer, up_low, kept):
        w_cd, w_gate, w_last = weights[layer]
        gain_pre, taps, conv_bias, bias_dt, log_rate, skip, gain_gate = small_of(layer)
        hidden, scale, normed_low, cd, edge, gate, pre, act, step, cum, entry, mixed, gated_low = kept
        reduced_out = reduce_weight(gated_low, up_low)
        grad_gated = times_back([(up_low, w_last)], w_last)
        grad_mixed, grad_gate, grad_gain_gate, message = call(
            gate_back_kernel,
            [
                ((rows, DI), F32),
                ((rows, DI), BF16),
                ((1, DI), F32),
                ((N, MESSAGE), BF16),
            ],
            [((rows, DI), F32)],
            place,
            grad_gated,
            mixed,
            gate,
            gain_gate,
            cum,
            act,
        )
        leaving = exchange_states(message, True)
        reduced_gate = reduce_weight(normed_low, grad_gate)
        grad_scaled, grad_bc, grad_cum = call(
            intra_back_kernel,
            [((rows, DI), F32), ((rows, 2 * N), F32), ((rows, H), F32)],
            [((rows, rows), F32), ((H, rows), F32)],
            place,
            act,
            step,
            cum,
            grad_mixed,
            entry,
        )
        grad_cd, grad_tail, grad_edge, grad_taps, grad_conv_bias, grad_heads = call(
            finish_kernel,
            [
                ((rows, DCD), BF16),
                ((EDGE, DCONV), F32),
                ((EDGE, DCONV), F32),
                ((K, DCONV), F32),
                ((1, DCONV), F32),
                ((EDGE, H), F32),
            ],
            [((rows, DCONV), F32)],
            place,
            cd,
            edge,
            pre,
            act,
            step,
            cum,
            grad_mixed,
            grad_scaled,
            grad_bc,
            grad_cum,
            entry,
            leaving,
            taps,
            bias_dt,
            log_rate,
            skip,
        )
        edge_back = from_behind(grad_edge, "seq", -1)
        grad_cd = lax.dynamic_update_slice(
            grad_cd, (grad_tail + edge_back).astype(BF16), (rows - EDGE, 0)
        )
        grad_normed = times_back([(grad_cd, w_cd), (grad_gate, w_gate)], w_cd)
        grad_pulled = grad_normed * gain_pre
        cross = jnp.mean(grad_pulled * hidden, axis=-1, keepdims=True)
        grad_hidden = up_low.astype(F32) + scale * grad_pulled - scale**3 * cross * hidden
        grad_gain_pre = jnp.sum(grad_normed * hidden * scale, axis=0)
        reduced_cd = reduce_weight(normed_low, grad_cd)
        small = (
            grad_gain_pre,
            grad_taps,
            grad_conv_bias,
            grad_heads[0],
            grad_heads[1],
            grad_heads[2],
            grad_gain_gate,
        )
        return grad_hidden, (reduced_cd, reduced_gate, reduced_out), small

    middle, kept_first = layer_forward(0, source)
    ending, kept_second = layer_forward(1, middle)
    grad_middle, large_second, small_second = layer_backward(1, upstream, kept_second)
    grad_middle_low = grad_middle.astype(BF16)
    grad_source, large_first, small_first = layer_backward(0, grad_middle_low, kept_first)

    is_first = section == 0

    def placed(first, second):
        keep = jnp.where(is_first, first, second)
        get = turned(jnp.where(is_first, second, first), "section", 1)
        return jnp.stack([jnp.where(is_first, keep, get), jnp.where(is_first, get, keep)])

    acts = placed(middle, ending).reshape(1, batches, 1, rows, D)
    in_keep = jnp.where(is_first, grad_source, grad_middle_low.astype(F32))
    in_get = turned(
        jnp.where(is_first, grad_middle_low, grad_source.astype(BF16)), "section", 1
    ).astype(F32)
    in_grad = jnp.stack([jnp.where(is_first, in_keep, in_get), jnp.where(is_first, in_get, in_keep)])
    in_grad = in_grad.reshape(1, batches, 1, rows, D)

    def whole_weight(first, second):
        keep = jnp.where(is_first, first, second)
        get = turned(jnp.where(is_first, second, first), "section", 1)
        return jnp.where(
            is_first,
            jnp.concatenate([keep, get], axis=0),
            jnp.concatenate([get, keep], axis=0),
        ).astype(F32)

    part_cd, part_gate, part_out = [whole_weight(a, b) for a, b in zip(large_first, large_second)]
    part_in = jnp.concatenate([part_gate, part_cd], axis=1)

    flat_grads = jnp.stack(
        [jnp.concatenate([part.reshape(-1) for part in small]) for small in (small_first, small_second)]
    )
    summed_small = lax.psum(flat_grads, ("section", "seq", "wshard"))
    mine = lax.dynamic_index_in_dim(summed_small, section, keepdims=False)
    small_out, at = [], 0
    for part, shown in zip(small_first, small_parts):
        size = part.size
        piece = mine[at : at + size].reshape(part.shape)
        at += size
        width = shown.shape[-1]
        piece = lax.dynamic_slice_in_dim(piece, shard * width, width, piece.ndim - 1)
        small_out.append(piece.reshape(shown.shape))
    return (acts, in_grad, small_out[0], part_in[None], *small_out[1:], part_out[None])


def solution(mesh):
    placed = (
        P(None, "wshard", "seq", None),
        P(None, "wshard", "seq", None),
        P(None, "wshard"),
        P("section", "wshard"),
        P("section", "wshard", None),
        P("section", None, "wshard"),
        P("section", "wshard"),
        P("section", "wshard"),
        P("section", "wshard"),
        P("section", "wshard"),
        P("section", "wshard"),
        P("section", "wshard", None),
    )
    return jax.shard_map(
        on_device,
        mesh=mesh,
        in_specs=placed,
        out_specs=(
            P("section", None, "wshard", "seq", None),
            P("section", None, "wshard", "seq", None),
            P("section", "wshard"),
            P("section", "wshard", None),
            P("section", None, "wshard"),
            P("section", "wshard"),
            P("section", "wshard"),
            P("section", "wshard"),
            P("section", "wshard"),
            P("section", "wshard"),
            P("section", "wshard", None),
        ),
        check_vma=False,
    )
```

time: 1840 us -> 894 us (0.49)
  waiting for transfers between devices: 857 us -> 438 us
  matrix products: 367 us -> 130 us
  other arithmetic: 261 us -> 50.8 us
  blocking collectives: 190 us -> 0 us
  Pallas kernels: 0 us -> 120 us
  local copies, waits for them, and re-layouts: 109 us -> 56.2 us
  starting transfers between devices: 23.9 us -> 70.4 us
    all_gather x8 -> x0, waiting for transfers between devices: 517 us -> none  [the longest x3 285 us: carried_in(): gathered = jax.tree.map(lambda a: lax.all_gather(a, axis), part)]
    dot_general x81 -> x48, matrix products: 367 us -> 130 us  [the longest x24 61.9 us: weight_terms(): lax.dot_general(lax.dynamic_slice_in_dim(low, at * size + which * half, h...]
    all_gather x10 -> x0, blocking collectives: 145 us -> none  [the longest x3 63.9 us: carried_in(): gathered = jax.tree.map(lambda a: lax.all_gather(a, axis), part)]
    ppermute x0 -> x32, waiting for transfers between devices: none -> 131 us  [turned(): lax.ppermute(block, axis, [(i, (i + distance) % count) for i in range(cou...]
    pallas_call x0 -> x16, Pallas kernels: none -> 120 us  [call(): pl.pallas_call(body, out_shape=[jax.ShapeDtypeStruct(shape, kind) for sha...]
    reduce_scatter x2 -> x0, waiting for transfers between devices: 84.6 us -> none  [the longest x1 84.6 us: on_device(): lax.psum_scatter(grad_proj_w[None].astype(jnp.bfloat16), 'wshard', scatte...]
    psum x1 -> x2, waiting for transfers between devices: 181 us -> 265 us  [the longest x1 230 us: reduce_weight(): return lax.psum(total.astype(BF16), 'seq')]
    reduce_sum x34 -> x3, other arithmetic: 63 us -> 1.63 us  [the longest x2 1.45 us: layer_backward(): grad_gain_pre = jnp.sum(grad_normed * hidden * scale, axis=0)]
  transfers between devices with their start and end apart: 28 -> 47, of which waited for: 18 -> 15; matrix products, arithmetic and copies ran while one was open for 18% -> 24% of each run, Pallas kernels for 0% -> 10%
where the time goes in v1:
time: 894 us; the launch traced here: 880 us
  waiting for transfers between devices  438 us (49%)
  matrix products  130 us (15%)
  Pallas kernels  120 us (13%)
  starting transfers between devices  70.4 us (8%)
  local copies, waits for them, and re-layouts  56.2 us (6%)
  other arithmetic  50.8 us (6%)
  between operations  15.6 us (2%)
    psum x1, waiting for transfers between devices, reduce_weight(): return lax.psum(total.astype(BF16), 'seq')  230 us
    ppermute x32, waiting for transfers between devices, turned(): lax.ppermute(block, axis, [(i, (i + distance) % count) for i in range(cou...  131 us
    pallas_call x16, Pallas kernels, call(): pl.pallas_call(body, out_shape=[jax.ShapeDtypeStruct(shape, kind) for sha...  120 us
    dot_general x24, matrix products, weight_terms(): lax.dot_general(lax.dynamic_slice_in_dim(low, at * size + which * half, h...  61.9 us
    psum x1, waiting for transfers between devices, on_device(): summed_small = lax.psum(flat_grads, ('section', 'seq', 'wshard'))  34.3 us
    dot_general x12, matrix products, times_back(): lax.dot_general(low, blocks_now[columns], (((1,), (1,)), ((), ())), prefe...  34 us
    dot_general x12, matrix products, times(): term = jnp.dot(part, block, preferred_element_type=F32)  33.7 us
    unnamed x4, waiting for transfers between devices  29.4 us
  transfers between devices with their start and end apart: 47, of which 15 were waited for; matrix products, arithmetic and copies ran while one was open for 24% of the time, Pallas kernels for 10%

profile of v1, /device:TPU:0, one launch (start us, length us, event | category | flops | bytes accessed | tf_op | source)
XLA Modules:
  0.0 879.7 jit_solution(7260698384894194101)
XLA Ops:
  28.7 29.3 %all-reduce.8.cloned.1.call-done = f32[29376]{0:T(1024)} async-done(((f32[29376]{0:T(1024)}), f32[29376]{0:T(1024)}) %all-reduce.8.cloned.1.call-update) | async-done | bytes 117520
  59.0 9.4 %collective-permute-done.1 = bf16[512,2336]{0,1:T(8,128)(2,1)S(1)} collective-permute-done((bf16[512,2336]{0,1:T(8,128)(2,1)}, bf16[512,2336]{0,1:T(8,128)(2,1)S(1)}, u32[]{:S(2)}, u32[]{:S(2)}) %collective-permute-start.1) | collective-permute-done | bytes 2392096 | tf_op jit(solution)/shard_map/ppermute | solution.py:396
  71.2 42.3 %collective-permute-done.5 = bf16[512,2048]{1,0:T(8,128)(2,1)} collective-permute-done((bf16[512,2048]{1,0:T(8,128)(2,1)}, bf16[512,2048]{1,0:T(8,128)(2,1)}, u32[]{:S(2)}, u32[]{:S(2)}) %collective-permute-start.5) | collective-permute-done | bytes 2097184 | tf_op jit(solution)/shard_map/ppermute | solution.py:396
  127.9 7.8 shard_map.203
  135.7 5.6 all-to-all-start
  141.2 16.4 %collective-permute-done.8 = bf16[1024,1024]{1,0:T(8,128)(2,1)} collective-permute-done((bf16[1024,1024]{1,0:T(8,128)(2,1)}, bf16[1024,1024]{1,0:T(8,128)(2,1)}, u32[]{:S(2)}, u32[]{:S(2)}) %collective-permute-start.8) | collective-permute-done | bytes 2097184 | tf_op jit(solution)/shard_map/ppermute | solution.py:396
  160.7 6.2 all-to-all-start.1
  174.3 8.0 shard_map.205.local
  183.1 6.0 shard_map.206
  199.6 4.5 collective-permute-start.10
  209.4 7.8 shard_map.207
  223.0 4.2 fusion.44
  230.5 6.3 all-to-all-done.2.gathered_ref
  254.4 8.0 shard_map.209.local
  263.2 5.9 shard_map.210
  269.1 7.9 shard_map.211
  277.0 11.3 %shard_map.212 = (f32[256,2048]{1,0:T(8,128)}, f32[256,256]{1,0:T(8,128)}, f32[256,32]{1,0:T(8,128)}) custom-call(s32[2]{0:T(128)} %pad_add_fusion.place, f32[256,2304]{1,0:T(8,128)} %get-tuple-element.57.act, f32[256,32]{1,0:T(8,128)} %get-tuple-element.58.step, f32[256,32]{1,0:T(8,128)} %get-tuple-element.59.cum, ...), custom_call_target="tpu_custom_call" | custom-call | tf_op jit(solution)/shard_map/pallas_call | solution.py:384
  288.3 6.0 all-to-all-start.4
  311.4 6.2 all-to-all-start.5
  332.3 14.6 %shard_map.214 = (bf16[256,2336]{1,0:T(8,128)(2,1)}, f32[8,2304]{1,0:T(8,128)}, f32[8,2304]{1,0:T(8,128)}, f32[4,2304]{1,0:T(4,128)}, f32[1,2304]{1,0:T(1,128)}, /*index=5*/f32[8,32]{1,0:T(8,128)}) custom-call(s32[2]{0:T(128)} %pad_add_fusion.place, f32[256,2336]{1,0:T(8,128)} %copy-done.3, f32[8,2304]{1,0:T(8,128)} %collective-permute-done.10.edge, ...), custom_call_target="tpu_custom_call" | custom-call | tf_op jit(solution)/shard_map/pallas_call | solution.py:384
  369.9 7.9 shard_map.215
  380.6 4.6 all-to-all-start.6
  401.5 10.8 %shard_map.216 = (f32[256,2048]{1,0:T(8,128)}, f32[256,256]{1,0:T(8,128)}, f32[256,32]{1,0:T(8,128)}) custom-call(s32[2]{0:T(128)} %pad_add_fusion.place, f32[256,2304]{1,0:T(8,128)} %get-tuple-element.52.act, f32[256,32]{1,0:T(8,128)} %get-tuple-element.53.step, f32[256,32]{1,0:T(8,128)} %get-tuple-element.54.cum, ...), custom_call_target="tpu_custom_call" | custom-call | tf_op jit(solution)/shard_map/pallas_call | solution.py:384
  419.1 5.6 all-to-all-start.7
  440.0 14.6 %shard_map.218 = (bf16[256,2336]{1,0:T(8,128)(2,1)}, f32[8,2304]{1,0:T(8,128)}, f32[8,2304]{1,0:T(8,128)}, f32[4,2304]{1,0:T(4,128)}, f32[1,2304]{1,0:T(1,128)}, /*index=5*/f32[8,32]{1,0:T(8,128)}) custom-call(s32[2]{0:T(128)} %pad_add_fusion.place, f32[256,2336]{1,0:T(8,128)} %copy-done.2, f32[8,2304]{1,0:T(8,128)} %copy-done.41, ...), custom_call_target="tpu_custom_call" | custom-call | tf_op jit(solution)/shard_map/pallas_call | solution.py:384
  487.4 15.5 %collective-permute-done.31 = bf16[512,1024]{1,0:T(8,128)(2,1)} collective-permute-done((bf16[512,1024]{1,0:T(8,128)(2,1)}, bf16[512,1024]{1,0:T(8,128)(2,1)}, u32[]{:S(2)}, u32[]{:S(2)}) %collective-permute-start.31) | collective-permute-done | bytes 1048608 | tf_op jit(solution)/shard_map/ppermute | solution.py:396
  506.0 22.7 %collective-permute-done.27 = bf16[256,2336]{0,1:T(8,128)(2,1)} collective-permute-done((bf16[256,2336]{0,1:T(8,128)(2,1)}, bf16[256,2336]{0,1:T(8,128)(2,1)}, u32[]{:S(2)}, u32[]{:S(2)}) %collective-permute-start.27) | collective-permute-done | bytes 1196064 | tf_op jit(solution)/shard_map/ppermute | solution.py:396
  532.1 22.1 %collective-permute-done.24 = bf16[256,2336]{0,1:T(8,128)(2,1)} collective-permute-done((bf16[256,2336]{0,1:T(8,128)(2,1)}, bf16[256,2336]{0,1:T(8,128)(2,1)}, u32[]{:S(2)}, u32[]{:S(2)}) %collective-permute-start.24) | collective-permute-done | bytes 1196064 | tf_op jit(solution)/shard_map/ppermute | solution.py:396
  570.7 34.3 %all-reduce.6.cloned.1.call-done = f32[2,14688]{1,0:T(2,128)} async-done(((f32[2,14688]{1,0:T(2,128)}), f32[2,14688]{1,0:T(2,128)}) %all-reduce.6.cloned.1.call-update) | async-done | bytes 117520 | tf_op jit(solution)/shard_map/psum | solution.py:701
  606.4 230.2 %all-reduce.10.cloned.1.call-done = (bf16[256,2336]{0,1:T(8,128)(2,1)}, bf16[256,2336]{0,1:T(8,128)(2,1)}, bf16[256,2048]{1,0:T(8,128)(2,1)}, bf16[256,2048]{1,0...) async-done(((bf16[256,2336]{0,1:T(8,128)(2,1)}, bf16[256,2336]{0,1:T(8,128)(2,1)}, bf16[256,2048]{1,0:T(8,128)(2,1)}, bf16[256,2048]{1,0:T(8,128)(2,1)}, ...) | async-done | bytes 6586384 | tf_op jit(solution)/shard_map/psum | solution.py:577
  860.5 5.5 fusion.13
  868.1 4.9 fusion
  (356 shorter events, 271.5 us)
Async XLA Ops:
  7.2 50.8 %all-reduce.8.cloned.1.call-start = ((), (), s32[]{:S(2)}) async-start(), calls=%async_computation.9 | async-start | bytes 237568
  10.5 58.0 %collective-permute-start.1 = (bf16[512,2336]{0,1:T(8,128)(2,1)}, bf16[512,2336]{0,1:T(8,128)(2,1)S(1)}, u32[]{:S(2)}, u32[]{:S(2)}) collective-permute-start(bf16[512,2336]{0,1:T(8,128)(2,1)} %slice_bitcast_fusion), channel_id=1, source_target_pairs={{0,1},{1,0},{2,3},{3,2},{4,5},{5,4},{6,7},{7,6},{8,9},{9,8},{10,11... | collective-permute-start | bytes 7176200 | tf_op jit(solution)/shard_map/ppermute | solution.py:396
  20.6 147.6 %collective-permute-start.4 = (bf16[512,2048]{1,0:T(8,128)(2,1)}, bf16[512,2048]{1,0:T(8,128)(2,1)}, u32[]{:S(2)}, u32[]{:S(2)}) collective-permute-start(bf16[512,2048]{1,0:T(8,128)(2,1)} %bitcast.15), channel_id=1, source_target_pairs={{0,16},{16,0},{1,17},{17,1},{2,18},{18,2},{3,19},{19,3},{4,20},{20... | collective-permute-start | bytes 6291464 | tf_op jit(solution)/shard_map/ppermute | solution.py:396
  20.6 92.9 %collective-permute-start.5 = (bf16[512,2048]{1,0:T(8,128)(2,1)}, bf16[512,2048]{1,0:T(8,128)(2,1)}, u32[]{:S(2)}, u32[]{:S(2)}) collective-permute-start(bf16[512,2048]{1,0:T(8,128)(2,1)} %bitcast.15), channel_id=1, source_target_pairs={{0,1},{1,0},{2,3},{3,2},{4,5},{5,4},{6,7},{7,6},{8,9},{9,8},{10,11... | collective-permute-start | bytes 6291464 | tf_op jit(solution)/shard_map/ppermute | solution.py:396
  20.6 92.9 %collective-permute-start = (bf16[512,2336]{0,1:T(8,128)(2,1)}, bf16[512,2336]{0,1:T(8,128)(2,1)}, u32[]{:S(2)}, u32[]{:S(2)}) collective-permute-start(bf16[512,2336]{0,1:T(8,128)(2,1)} %slice_bitcast_fusion), channel_id=1, source_target_pairs={{0,16},{16,0},{1,17},{17,1},{2,18},{18,2},{3,19},{19,3},{4,20},{20... | collective-permute-start | bytes 7176200 | tf_op jit(solution)/shard_map/ppermute | solution.py:396
  24.8 132.8 %collective-permute-start.8 = (bf16[1024,1024]{1,0:T(8,128)(2,1)}, bf16[1024,1024]{1,0:T(8,128)(2,1)}, u32[]{:S(2)}, u32[]{:S(2)}) collective-permute-start(bf16[1024,1024]{1,0:T(8,128)(2,1)} %bitcast.229), channel_id=1, source_target_pairs={{0,1},{1,0},{2,3},{3,2},{4,5},{5,4},{6,7},{7,6},{8,9},{9,8},{10,11... | collective-permute-start | bytes 6291464 | tf_op jit(solution)/shard_map/ppermute | solution.py:396
  68.5 48.2 %collective-permute-start.2 = (bf16[512,2336]{0,1:T(8,128)(2,1)S(1)}, bf16[512,2336]{0,1:T(8,128)(2,1)S(1)}, u32[]{:S(2)}, u32[]{:S(2)}) collective-permute-start(bf16[512,2336]{0,1:T(8,128)(2,1)S(1)} %collective-permute-done.1), channel_id=1, source_target_pairs={{0,16},{16,0},{1,17},{17,1},{2,18},{18,2},{3,19},{19,3},{4,20},{20... | collective-permute-start | bytes 7176200 | tf_op jit(solution)/shard_map/ppermute | solution.py:396
  113.5 75.6 %collective-permute-start.7 = (bf16[1024,1024]{1,0:T(8,128)(2,1)}, bf16[1024,1024]{1,0:T(8,128)(2,1)}, u32[]{:S(2)}, u32[]{:S(2)}) collective-permute-start(bf16[1024,1024]{1,0:T(8,128)(2,1)} %bitcast.230), channel_id=1, source_target_pairs={{0,16},{16,0},{1,17},{17,1},{2,18},{18,2},{3,19},{19,3},{4,20},{20... | collective-permute-start | bytes 6291464 | tf_op jit(solution)/shard_map/ppermute | solution.py:396
  113.5 57.0 %collective-permute-start.6 = (bf16[512,2048]{1,0:T(8,128)(2,1)}, bf16[512,2048]{1,0:T(8,128)(2,1)}, u32[]{:S(2)}, u32[]{:S(2)}) collective-permute-start(bf16[512,2048]{1,0:T(8,128)(2,1)} %collective-permute-done.5), channel_id=1, source_target_pairs={{0,16},{16,0},{1,17},{17,1},{2,18},{18,2},{3,19},{19,3},{4,20},{20... | collective-permute-start | bytes 6291464 | tf_op jit(solution)/shard_map/ppermute | solution.py:396
  157.6 33.5 %collective-permute-start.9 = (bf16[1024,1024]{1,0:T(8,128)(2,1)}, bf16[1024,1024]{1,0:T(8,128)(2,1)}, u32[]{:S(2)}, u32[]{:S(2)}) collective-permute-start(bf16[1024,1024]{1,0:T(8,128)(2,1)} %collective-permute-done.8), channel_id=1, source_target_pairs={{0,16},{16,0},{1,17},{17,1},{2,18},{18,2},{3,19},{19,3},{4,20},{20... | collective-permute-start | bytes 6291464 | tf_op jit(solution)/shard_map/ppermute | solution.py:396
  296.8 24.5 %collective-permute-start.33 = (bf16[512,1024]{1,0:T(8,128)(2,1)}, bf16[512,1024]{1,0:T(8,128)(2,1)}, u32[]{:S(2)}, u32[]{:S(2)}) collective-permute-start(bf16[512,1024]{1,0:T(8,128)(2,1)} %convolution_convert_fusion.8), channel_id=1, source_target_pairs={{0,16},{16,0},{1,17},{17,1},{2,18},{18,2},{3,19},{19,3},{4,20},{20... | collective-permute-start | bytes 3145736 | tf_op jit(solution)/shard_map/ppermute | solution.py:396
  299.3 99.6 %collective-permute-start.32 = (bf16[512,1024]{1,0:T(8,128)(2,1)}, bf16[512,1024]{1,0:T(8,128)(2,1)}, u32[]{:S(2)}, u32[]{:S(2)}) collective-permute-start(bf16[512,1024]{1,0:T(8,128)(2,1)} %convolution_convert_fusion.9), channel_id=1, source_target_pairs={{0,16},{16,0},{1,17},{17,1},{2,18},{18,2},{3,19},{19,3},{4,20},{20... | collective-permute-start | bytes 3145736 | tf_op jit(solution)/shard_map/ppermute | solution.py:396
  301.3 123.5 %collective-permute-start.18 = (bf16[256,2048]{1,0:T(8,128)(2,1)}, bf16[256,2048]{1,0:T(8,128)(2,1)}, u32[]{:S(2)}, u32[]{:S(2)}) collective-permute-start(bf16[256,2048]{1,0:T(8,128)(2,1)} %convolution_convert_fusion.5), channel_id=1, source_target_pairs={{0,16},{16,0},{1,17},{17,1},{2,18},{18,2},{3,19},{19,3},{4,20},{20... | collective-permute-start | bytes 3145736 | tf_op jit(solution)/shard_map/ppermute | solution.py:396
  302.7 22.8 %collective-permute-start.19 = (bf16[256,2048]{1,0:T(8,128)(2,1)}, bf16[256,2048]{1,0:T(8,128)(2,1)}, u32[]{:S(2)}, u32[]{:S(2)}) collective-permute-start(bf16[256,2048]{1,0:T(8,128)(2,1)} %convolution_convert_fusion.4), channel_id=1, source_target_pairs={{0,16},{16,0},{1,17},{17,1},{2,18},{18,2},{3,19},{19,3},{4,20},{20... | collective-permute-start | bytes 3145736 | tf_op jit(solution)/shard_map/ppermute | solution.py:396
  324.2 88.9 %collective-permute-start.34 = (bf16[512,1024]{1,0:T(8,128)(2,1)}, bf16[512,1024]{1,0:T(8,128)(2,1)}, u32[]{:S(2)}, u32[]{:S(2)}) collective-permute-start(bf16[512,1024]{1,0:T(8,128)(2,1)} %add_convert_fusion.1), channel_id=1, source_target_pairs={{0,1},{1,0},{2,3},{3,2},{4,5},{5,4},{6,7},{7,6},{8,9},{9,8},{10,11... | collective-permute-start | bytes 3145736 | tf_op jit(solution)/shard_map/ppermute | solution.py:396
  328.2 96.8 %collective-permute-start.20 = (bf16[256,2048]{1,0:T(8,128)(2,1)}, bf16[256,2048]{1,0:T(8,128)(2,1)}, u32[]{:S(2)}, u32[]{:S(2)}) collective-permute-start(bf16[256,2048]{1,0:T(8,128)(2,1)} %fusion.12), channel_id=1, source_target_pairs={{0,1},{1,0},{2,3},{3,2},{4,5},{5,4},{6,7},{7,6},{8,9},{9,8},{10,11... | collective-permute-start | bytes 3145736 | tf_op jit(solution)/shard_map/ppermute | solution.py:396
  380.6 48.2 %collective-permute-start.16 = (bf16[256,2048]{1,0:T(8,128)(2,1)}, bf16[256,2048]{1,0:T(8,128)(2,1)}, u32[]{:S(2)}, u32[]{:S(2)}) collective-permute-start(bf16[256,2048]{1,0:T(8,128)(2,1)} %convolution_convert_fusion.6), channel_id=1, source_target_pairs={{0,16},{16,0},{1,17},{17,1},{2,18},{18,2},{3,19},{19,3},{4,20},{20... | collective-permute-start | bytes 3145736 | tf_op jit(solution)/shard_map/ppermute | solution.py:396
  380.6 36.1 %all-to-all-start.6 = ((bf16[8,16,2176]{2,1,0:T(8,128)(2,1)}), bf16[8,16,2176]{2,1,0:T(8,128)(2,1)}, u32[]{:S(2)}, u32[]{:S(2)}) async-start(bf16[8,16,2176]{2,1,0:T(8,128)(2,1)} %bitcast.201), calls=%async_computation.6 | async-start | bytes 1114112 | tf_op jit(solution)/shard_map/all_to_all | solution.py:409
  398.8 32.9 %collective-permute-start.30 = (bf16[512,1024]{1,0:T(8,128)(2,1)}, bf16[512,1024]{1,0:T(8,128)(2,1)}, u32[]{:S(2)}, u32[]{:S(2)}) collective-permute-start(bf16[512,1024]{1,0:T(8,128)(2,1)} %convolution_convert_fusion.10), channel_id=1, source_target_pairs={{0,16},{16,0},{1,17},{17,1},{2,18},{18,2},{3,19},{19,3},{4,20},{20... | collective-permute-start | bytes 3145736 | tf_op jit(solution)/shard_map/ppermute | solution.py:396
  413.0 22.9 %collective-permute-start.26 = (bf16[256,2336]{0,1:T(8,128)(2,1)}, bf16[256,2336]{0,1:T(8,128)(2,1)}, u32[]{:S(2)}, u32[]{:S(2)}) collective-permute-start(bf16[256,2336]{0,1:T(8,128)(2,1)} %convolution_convert_fusion), channel_id=1, source_target_pairs={{0,16},{16,0},{1,17},{17,1},{2,18},{18,2},{3,19},{19,3},{4,20},{20... | collective-permute-start | bytes 3588104 | tf_op jit(solution)/shard_map/ppermute | solution.py:396
  424.7 180.2 %all-reduce.6.cloned.1.call-start = ((), (), s32[]{:S(2)}) async-start(), calls=%async_computation.8 | async-start | bytes 235520 | tf_op jit(solution)/shard_map/psum | solution.py:701
  424.8 56.0 %collective-permute-start.29 = (bf16[512,1024]{1,0:T(8,128)(2,1)}, bf16[512,1024]{1,0:T(8,128)(2,1)}, u32[]{:S(2)}, u32[]{:S(2)}) collective-permute-start(bf16[512,1024]{1,0:T(8,128)(2,1)} %convolution_convert_fusion.11), channel_id=1, source_target_pairs={{0,16},{16,0},{1,17},{17,1},{2,18},{18,2},{3,19},{19,3},{4,20},{20... | collective-permute-start | bytes 3145736 | tf_op jit(solution)/shard_map/ppermute | solution.py:396
  425.1 56.4 %collective-permute-start.15 = (bf16[256,2048]{1,0:T(8,128)(2,1)}, bf16[256,2048]{1,0:T(8,128)(2,1)}, u32[]{:S(2)}, u32[]{:S(2)}) collective-permute-start(bf16[256,2048]{1,0:T(8,128)(2,1)} %convolution_convert_fusion.7), channel_id=1, source_target_pairs={{0,16},{16,0},{1,17},{17,1},{2,18},{18,2},{3,19},{19,3},{4,20},{20... | collective-permute-start | bytes 3145736 | tf_op jit(solution)/shard_map/ppermute | solution.py:396
  428.8 77.2 %collective-permute-start.25 = (bf16[256,2336]{0,1:T(8,128)(2,1)}, bf16[256,2336]{0,1:T(8,128)(2,1)}, u32[]{:S(2)}, u32[]{:S(2)}) collective-permute-start(bf16[256,2336]{0,1:T(8,128)(2,1)} %convolution_convert_fusion.1), channel_id=1, source_target_pairs={{0,16},{16,0},{1,17},{17,1},{2,18},{18,2},{3,19},{19,3},{4,20},{20... | collective-permute-start | bytes 3588104 | tf_op jit(solution)/shard_map/ppermute | solution.py:396
  431.7 49.7 %collective-permute-start.17 = (bf16[256,2048]{1,0:T(8,128)(2,1)}, bf16[256,2048]{1,0:T(8,128)(2,1)}, u32[]{:S(2)}, u32[]{:S(2)}) collective-permute-start(bf16[256,2048]{1,0:T(8,128)(2,1)} %fusion.11), channel_id=1, source_target_pairs={{0,1},{1,0},{2,3},{3,2},{4,5},{5,4},{6,7},{7,6},{8,9},{9,8},{10,11... | collective-permute-start | bytes 3145736 | tf_op jit(solution)/shard_map/ppermute | solution.py:396
  476.4 26.5 %collective-permute-start.31 = (bf16[512,1024]{1,0:T(8,128)(2,1)}, bf16[512,1024]{1,0:T(8,128)(2,1)}, u32[]{:S(2)}, u32[]{:S(2)}) collective-permute-start(bf16[512,1024]{1,0:T(8,128)(2,1)} %add_convert_fusion.3), channel_id=1, source_target_pairs={{0,1},{1,0},{2,3},{3,2},{4,5},{5,4},{6,7},{7,6},{8,9},{9,8},{10,11... | collective-permute-start | bytes 3145736 | tf_op jit(solution)/shard_map/ppermute | solution.py:396
  480.8 47.9 %collective-permute-start.27 = (bf16[256,2336]{0,1:T(8,128)(2,1)}, bf16[256,2336]{0,1:T(8,128)(2,1)}, u32[]{:S(2)}, u32[]{:S(2)}) collective-permute-start(bf16[256,2336]{0,1:T(8,128)(2,1)} %fusion.6), channel_id=1, source_target_pairs={{0,1},{1,0},{2,3},{3,2},{4,5},{5,4},{6,7},{7,6},{8,9},{9,8},{10,11... | collective-permute-start | bytes 3588104 | tf_op jit(solution)/shard_map/ppermute | solution.py:396
  481.4 50.7 %collective-permute-start.22 = (bf16[256,2336]{0,1:T(8,128)(2,1)}, bf16[256,2336]{0,1:T(8,128)(2,1)}, u32[]{:S(2)}, u32[]{:S(2)}) collective-permute-start(bf16[256,2336]{0,1:T(8,128)(2,1)} %convolution_convert_fusion.3), channel_id=1, source_target_pairs={{0,16},{16,0},{1,17},{17,1},{2,18},{18,2},{3,19},{19,3},{4,20},{20... | collective-permute-start | bytes 3588104 | tf_op jit(solution)/shard_map/ppermute | solution.py:396
  481.4 72.8 %collective-permute-start.24 = (bf16[256,2336]{0,1:T(8,128)(2,1)}, bf16[256,2336]{0,1:T(8,128)(2,1)}, u32[]{:S(2)}, u32[]{:S(2)}) collective-permute-start(bf16[256,2336]{0,1:T(8,128)(2,1)} %fusion.4), channel_id=1, source_target_pairs={{0,1},{1,0},{2,3},{3,2},{4,5},{5,4},{6,7},{7,6},{8,9},{9,8},{10,11... | collective-permute-start | bytes 3588104 | tf_op jit(solution)/shard_map/ppermute | solution.py:396
  483.7 353.0 %all-reduce.10.cloned.1.call-start = ((), (), s32[]{:S(2)}) async-start(), calls=%async_computation.10 | async-start | bytes 13172736 | tf_op jit(solution)/shard_map/psum | solution.py:577
  570.5 279.7 %collective-permute-start.14 = (bf16[256,1024]{1,0:T(8,128)(2,1)}, bf16[256,1024]{1,0:T(8,128)(2,1)}, u32[]{:S(2)}, u32[]{:S(2)}) collective-permute-start(bf16[256,1024]{1,0:T(8,128)(2,1)} %convert_select_fusion.3), channel_id=1, source_target_pairs={{0,16},{16,0},{1,17},{17,1},{2,18},{18,2},{3,19},{19,3},{4,20},{20... | collective-permute-start | bytes 1572872 | tf_op jit(solution)/shard_map/ppermute | solution.py:396
  843.4 22.6 %collective-permute-start.28 = (bf16[256,2336]{0,1:T(8,128)(2,1)}, bf16[256,2336]{0,1:T(8,128)(2,1)}, u32[]{:S(2)}, u32[]{:S(2)}) collective-permute-start(bf16[256,2336]{0,1:T(8,128)(2,1)} %get-tuple-element.115), channel_id=1, source_target_pairs={{0,16},{16,0},{1,17},{17,1},{2,18},{18,2},{3,19},{19,3},{4,20},{20... | collective-permute-start | bytes 3588104 | tf_op jit(solution)/shard_map/ppermute | solution.py:396
  (87 other events, 989.8 us)
Sparse Core Ops, SparseCore 0:
  24.9 33.0 all-reduce.7
  483.8 121.1 all-reduce.5
  612.1 224.4 all-reduce.9
